TPU v7x, 256 devices: a whole 4x4x8 slice. The times are simulated.
256 devices in a mesh: pop: 32 (over y_lo, z, core), fsdp: 8 (over y_hi, x).
Axes of the slice: x: 4, y: 4 (y_hi: 2, y_lo: 2; y = y_hi * 2 + y_lo), z: 8, core: 2. Of those that a mesh axis runs over, the one named last changes fastest.
Arguments:
- tokens: bfloat16 [28672, 4096], P('pop', 'fsdp'), may hold values from -6 to 6
- up_weight: bfloat16 [4096, 14336], P('pop', 'fsdp'), may hold values from -0.09375 to 0.09375
- a_bank: bfloat16 [1024, 4096], P(None, 'pop'), may hold values from -6 to 6
- b_bank: bfloat16 [1024, 14336], P(None, 'fsdp'), may hold values from -6 to 6
- factor_index: int32 [64, 4], replicated, may hold values from 0 to 1023
- mirror: int32 [64], P('pop'), may hold values 0 or 1
- rewards: int32 [64], P('pop'), may hold values from -8 to 7
Outputs:
- hidden: bfloat16 [28672, 14336], P('pop', 'fsdp')
- update: float32 [4096, 14336], P('pop', 'fsdp')
All inputs are finite; a program needn't handle non-finite values. No bound on the sum of `mirror` on one device may be relied on, other than what follows from the above.
Results may differ from a plain program's by a relative error of at most 0.001.
Values may be sent and summed in bfloat16 or wider, within the bound.
A program may use at most 128 MiB of HBM per device.

v0:
```python
import math

import jax
import jax.numpy as jnp
from jax import lax
from jax.sharding import PartitionSpec as P

D = 4096
RANK = 4
SEQ = 448


noise_scale = 0.5


def sent_to_all(array, axis):
    copies = jnp.broadcast_to(array, (lax.axis_size(axis), *array.shape))
    return lax.all_to_all(copies, axis, split_axis=0, concat_axis=0, tiled=True)


def joined_along(parts, dim):
    parts = jnp.moveaxis(parts, 0, dim)
    dims = parts.shape
    return parts.reshape(*dims[:dim], dims[dim] * dims[dim + 1], *dims[dim + 2 :])


def gather_directly(array, axis, dim):
    parts = sent_to_all(array, axis)
    return joined_along(parts, dim)


def shaped_weights(rewards, mirror):
    members_all = rewards.shape[0]
    member_ids = jnp.arange(members_all)
    beaten = rewards[None, :] < rewards[:, None]
    level_tie = (rewards[None, :] == rewards[:, None]) & (member_ids[None, :] < member_ids[:, None])
    standing = jnp.sum((beaten | level_tie).astype(jnp.int32), axis=1)
    signed = (2 * mirror - 1).astype(jnp.float32)
    shaped = 2.0 * standing.astype(jnp.float32) / (members_all - 1) - 1.0
    return shaped * signed / math.sqrt(members_all * RANK)


def per_device(tokens, up_weight, a_bank, b_bank, factor_index, mirror, rewards):
    members_here = mirror.shape[0]
    own_width = members_here * RANK
    position = lax.axis_index("pop")
    flat_index = factor_index.reshape(-1)
    picked_a = jnp.take(a_bank, flat_index, axis=0)
    picked_b = jnp.take(b_bank, flat_index, axis=0)
    first_own = position * own_width
    gathered_a, rewards_all, mirror_all = (
        gather_directly(picked_a, "pop", 1),
        gather_directly(rewards, "pop", 0),
        gather_directly(mirror, "pop", 0),
    )
    own_a = lax.dynamic_slice_in_dim(gathered_a, first_own, own_width, 0)
    own_b = lax.dynamic_slice_in_dim(picked_b, first_own, own_width, 0).astype(jnp.float32)
    own_signs = (2 * mirror - 1).astype(jnp.float32)
    column_factor = jnp.repeat(noise_scale / math.sqrt(D * RANK) * own_signs, RANK)
    member_of_column = jnp.arange(own_width) // RANK
    row_count = tokens.shape[0]
    entire_weight = lax.all_gather(up_weight, "pop", axis=0, tiled=True)
    piece = lax.all_gather(tokens, "fsdp", axis=1, tiled=True)
    dense_sum = jnp.dot(piece, entire_weight, preferred_element_type=jnp.float32)
    low_sum = jnp.dot(piece, own_a.T, preferred_element_type=jnp.float32)
    member_of_row = jnp.arange(row_count) // SEQ
    same_member = member_of_row[:, None] == member_of_column[None, :]
    scaled = jnp.where(same_member, low_sum * column_factor[None, :], 0.0)
    perturbed = jnp.dot(scaled, own_b, precision=lax.Precision.HIGHEST)
    hidden = (dense_sum + perturbed).astype(jnp.bfloat16)
    weighting = shaped_weights(rewards_all, mirror_all)
    spread = jnp.repeat(weighting, RANK)
    update = jnp.dot(
        picked_a.astype(jnp.float32).T,
        spread[:, None] * picked_b.astype(jnp.float32),
        precision=lax.Precision.HIGHEST,
    )
    return (hidden, update)


def solution(mesh):
    in_specs = (
        P("pop", "fsdp"),
        P("pop", "fsdp"),
        P(None, "pop"),
        P(None, "fsdp"),
        P(),
        P("pop"),
        P("pop"),
    )
    out_specs = (P("pop", "fsdp"), P("pop", "fsdp"))
    return jax.shard_map(
        per_device, mesh=mesh, in_specs=in_specs, out_specs=out_specs, check_vma=False
    )
```

profile of v0, /device:TPU:17, one launch (start us, length us, event | category | flops | bytes accessed | tf_op | source)
XLA Modules:
  0.0 261.1 jit_solution(9321200983050298536)
XLA Ops:
  7.2 0.0 copy-start
  7.2 0.0 copy-start.1
  7.2 0.0 all-gather.3.cloned.1.call-start
  7.2 0.7 all-gather.3.cloned.1.call-update
  7.9 0.0 all-gather.5.cloned.1.call-start
  8.0 0.7 all-gather.5.cloned.1.call-update
  8.7 1.3 broadcast_in_dim.51
  9.9 10.0 %all-to-all-start.2 = ((s32[32,1,2]{2,1,0:T(1,128)}), s32[32,1,2]{2,1,0:T(1,128)S(1)}, u32[]{:S(2)}, u32[]{:S(2)}) async-start(s32[32,1,2]{2,1,0:T(1,128)} %broadcast_in_dim.51), calls=%async_computation.2 | async-start | bytes 32768 | tf_op jit(solution)/shard_map/all_to_all | solution.py:18
  20.0 0.8 copy.15
  20.7 0.1 reshape.94
  20.8 0.1 reshape.93
  21.0 0.0 copy-done
  21.0 0.9 gather_fusion
  21.9 5.9 %all-to-all-done.2 = s32[32,1,2]{2,1,0:T(1,128)S(1)} async-done(((s32[32,1,2]{2,1,0:T(1,128)}), s32[32,1,2]{2,1,0:T(1,128)S(1)}, u32[]{:S(2)}, u32[]{:S(2)}) %all-to-all-start.2) | async-done | bytes 288 | tf_op jit(solution)/shard_map/all_to_all | solution.py:18
  27.7 1.3 broadcast_in_dim.50
  29.0 4.3 %all-to-all-start.1 = ((s32[32,1,2]{2,1,0:T(1,128)}), s32[32,1,2]{2,1,0:T(1,128)S(1)}, u32[]{:S(2)}, u32[]{:S(2)}) async-start(s32[32,1,2]{2,1,0:T(1,128)} %broadcast_in_dim.50), calls=%async_computation.1 | async-start | bytes 32768 | tf_op jit(solution)/shard_map/all_to_all | solution.py:18
  33.3 0.1 broadcast_select_fusion.1
  33.4 0.1 copy.17
  33.5 7.6 %all-to-all-done.1 = s32[32,1,2]{2,1,0:T(1,128)S(1)} async-done(((s32[32,1,2]{2,1,0:T(1,128)}), s32[32,1,2]{2,1,0:T(1,128)S(1)}, u32[]{:S(2)}, u32[]{:S(2)}) %all-to-all-start.1) | async-done | bytes 288 | tf_op jit(solution)/shard_map/all_to_all | solution.py:18
  41.2 1.6 broadcast_in_dim.45
  42.7 4.5 %all-to-all-start = ((bf16[32,256,128]{1,2,0:T(8,128)(2,1)}), bf16[32,256,128]{1,2,0:T(8,128)(2,1)S(1)}, u32[]{:S(2)}, u32[]{:S(2)}) async-start(bf16[32,256,128]{1,2,0:T(8,128)(2,1)} %broadcast_in_dim.45), calls=%async_computation | async-start | bytes 4194304 | tf_op jit(solution)/shard_map/all_to_all | solution.py:18
  47.2 0.0 copy-done.1
  47.2 0.1 broadcast_in_dim.46
  47.3 0.1 mul.47
  47.4 5.6 %gather_fusion.1 = bf16[256,1792]{1,0:T(8,128)(2,1)} fusion(bf16[1024,1792]{1,0:T(8,128)(2,1)} %param.10, s32[1024]{0:T(1024)S(1)} %pad_clamp_fusion), kind=kCustom, calls=%fused_computation.1 | custom fusion | bytes 1836032 | tf_op jit(solution)/shard_map/jit(_take)/gather | solution.py:49
  53.0 1.3 broadcast_select_fusion
  54.3 0.1 convert_reduce_fusion.1
  54.4 0.1 convert_element_type.28
  54.5 0.5 broadcast.138
  55.0 0.7 reduce.7
  55.7 0.1 lt.62
  55.8 0.2 convert_reduce_fusion
  56.0 0.1 broadcast_in_dim.52
  56.1 0.1 mul.54
  56.2 1.9 fusion
  58.1 38.6 %all-to-all-done = bf16[32,256,128]{1,2,0:T(8,128)(2,1)S(1)} async-done(((bf16[32,256,128]{1,2,0:T(8,128)(2,1)}), bf16[32,256,128]{1,2,0:T(8,128)(2,1)S(1)}, u32[]{:S(2)}, u32[]{:S(2)}) %all-to-all-start) | async-done | bytes 2097184 | tf_op jit(solution)/shard_map/all_to_all | solution.py:18
  96.7 43.0 %all-gather.3.cloned.1.call-done = bf16[896,4096]{1,0:T(8,128)(2,1)} async-done(((bf16[896,512]{1,0:T(8,128)(2,1)}), bf16[896,4096]{1,0:T(8,128)(2,1)}) %all-gather.3.cloned.1.call-update) | async-done | bytes 7340048 | tf_op jit(solution)/shard_map/all_gather | solution.py:63
  139.7 5.6 %fusion.4 = f32[896,8]{0,1:T(8,128)S(1)} fusion(bf16[896,4096]{1,0:T(8,128)(2,1)} %all-gather.3.cloned.1.call-done, bf16[256,4096]{0,1:T(8,128)(2,1)S(1)} %bitcast.13, s32[]{:T(128)S(6)} %select_n.57, f32[8]{0:T(128)S(1)} %mul.47, s32[896]{0:T(1024)S(1)} %add_select_fusion, s32[8]{0:T(128)S(1)} %and_select_fusion), kind=kOutput, calls=%fused_computation.8 | convolution fusion | flops 58741760 | bytes 8422404 | tf_op jit(solution)/shard_map/dot_general | solution.py:65
  145.3 87.2 %all-gather.5.cloned.1.call-done = bf16[4096,1792]{1,0:T(8,128)(2,1)} async-done(((bf16[128,1792]{1,0:T(8,128)(2,1)}), bf16[4096,1792]{1,0:T(8,128)(2,1)}) %all-gather.5.cloned.1.call-update) | async-done | bytes 14680080 | tf_op jit(solution)/shard_map/all_gather | solution.py:62
  232.5 17.0 %fusion.15 = f32[896,1792]{1,0:T(8,128)S(1)} fusion(bf16[896,4096]{1,0:T(8,128)(2,1)} %all-gather.3.cloned.1.call-done, bf16[4096,1792]{1,0:T(8,128)(2,1)} %all-gather.5.cloned.1.call-done), kind=kOutput, calls=%fused_computation.38 | convolution fusion | flops 13153337344 | bytes 28442624 | tf_op jit(solution)/shard_map/dot_general | solution.py:64
  249.5 4.7 %add_convert_fusion = bf16[896,1792]{1,0:T(8,128)(2,1)} fusion(f32[896,1792]{1,0:T(8,128)S(1)} %fusion.15, f32[896,8]{0,1:T(8,128)S(1)} %fusion.4, bf16[256,1792]{1,0:T(8,128)(2,1)S(1)} %broadcast_select_fusion, s32[]{:T(128)S(6)} %select_n.57), kind=kOutput, calls=%fused_computation.2 | convolution fusion | flops 157351936 | bytes 9691140 | tf_op jit(solution)/shard_map/dot_general | solution.py:69
  (7 shorter events, 0.0 us)
Async XLA Ops:
  7.2 13.8 %copy-start = (bf16[1024,128]{1,0:T(8,128)(2,1)S(1)}, bf16[1024,128]{1,0:T(8,128)(2,1)}, u32[]{:S(2)}) copy-start(bf16[1024,128]{1,0:T(8,128)(2,1)} %param.9) | copy-start | bytes 786436
  7.2 40.0 %copy-start.1 = (s32[2]{0:T(128)S(1)}, s32[2]{0:T(128)}, u32[]{:S(2)}) copy-start(s32[2]{0:T(128)} %param.12) | copy-start | bytes 28
  7.2 132.5 %all-gather.3.cloned.1.call-start = ((), (), s32[]{:S(2)}) async-start(), calls=%async_computation.3 | async-start | bytes 8257536 | tf_op jit(solution)/shard_map/all_gather | solution.py:63
  7.9 224.6 %all-gather.5.cloned.1.call-start = ((), (), s32[]{:S(2)}) async-start(), calls=%async_computation.4 | async-start | bytes 15138816 | tf_op jit(solution)/shard_map/all_gather | solution.py:62
  9.9 17.8 %all-to-all-start.2 = ((s32[32,1,2]{2,1,0:T(1,128)}), s32[32,1,2]{2,1,0:T(1,128)S(1)}, u32[]{:S(2)}, u32[]{:S(2)}) async-start(s32[32,1,2]{2,1,0:T(1,128)} %broadcast_in_dim.51), calls=%async_computation.2 | async-start | bytes 32768 | tf_op jit(solution)/shard_map/all_to_all | solution.py:18
  29.0 12.2 %all-to-all-start.1 = ((s32[32,1,2]{2,1,0:T(1,128)}), s32[32,1,2]{2,1,0:T(1,128)S(1)}, u32[]{:S(2)}, u32[]{:S(2)}) async-start(s32[32,1,2]{2,1,0:T(1,128)} %broadcast_in_dim.50), calls=%async_computation.1 | async-start | bytes 32768 | tf_op jit(solution)/shard_map/all_to_all | solution.py:18
  42.7 54.0 %all-to-all-start = ((bf16[32,256,128]{1,2,0:T(8,128)(2,1)}), bf16[32,256,128]{1,2,0:T(8,128)(2,1)S(1)}, u32[]{:S(2)}, u32[]{:S(2)}) async-start(bf16[32,256,128]{1,2,0:T(8,128)(2,1)} %broadcast_in_dim.45), calls=%async_computation | async-start | bytes 4194304 | tf_op jit(solution)/shard_map/all_to_all | solution.py:18
Sparse Core Ops, SparseCore 0:
  10.5 129.1 all-gather.2
  141.6 90.8 all-gather.4
where the time goes:
time: 262 us; the launch traced here: 261 us
  waiting for transfers between devices  184 us (70%)
  matrix products  29.2 us (11%)
  starting transfers between devices  18.8 us (7%)
  between operations  14.2 us (5%)
  local copies, waits for them, and re-layouts  12.7 us (5%)
    all_gather x1, waiting for transfers between devices, per_device(): entire_weight = lax.all_gather(up_weight, 'pop', axis=0, tiled=True)  87.2 us
    all_to_all x3, waiting for transfers between devices, sent_to_all(): return lax.all_to_all(copies, axis, split_axis=0, concat_axis=0, tiled=True)  52.2 us
    all_gather x1, waiting for transfers between devices, per_device(): piece = lax.all_gather(tokens, 'fsdp', axis=1, tiled=True)  43 us
    all_to_all x3, starting transfers between devices, sent_to_all(): return lax.all_to_all(copies, axis, split_axis=0, concat_axis=0, tiled=True)  18.8 us
    dot_general x1, matrix products, per_device(): jnp.dot(piece, entire_weight, preferred_element_type=jnp.float32)  17 us
    dot_general x1, matrix products, per_device(): low_sum = jnp.dot(piece, own_a.T, preferred_element_type=jnp.float32)  5.63 us
    gather x1, local copies, waits for them, and re-layouts, per_device(): picked_b = jnp.take(b_bank, flat_index, axis=0)  5.58 us
  transfers between devices with their start and end apart: 5, of which 5 were waited for; matrix products, arithmetic and copies ran while one was open for 9% of the time, Pallas kernels for 0%

commit v1 on v0

v1 whole, which is shorter than its diff:
```python
import math

import jax
import jax.numpy as jnp
from jax import lax
from jax.experimental import pallas as pl
from jax.experimental.pallas import tpu as pltpu
from jax.sharding import PartitionSpec as P

D = 4096
RANK = 4
SEQ = 448
MEMBERS = 64
BANK = 1024
ROWS = 896
WIDTH = 1792
TILE = 256
TILES = WIDTH // TILE
PIECES = D // TILE
X, Z, CORES = 4, 8, 2
POP, FSDP = 32, 8
FACTORS = MEMBERS * RANK
SLOT = 128
LAST = 6

noise_scale = 0.5
MESH = pl.DeviceIdType.MESH


def picked(values, table):
    return jnp.dot(values.astype(jnp.bfloat16), table, preferred_element_type=jnp.float32)


def flat_rows(index, rows, first, period):
    row = lax.broadcasted_iota(jnp.int32, (rows, MEMBERS), 0)
    factor = first + lax.rem(row, period)
    chosen = lax.broadcasted_iota(jnp.int32, (rows, MEMBERS), 1) == lax.div(factor, RANK)
    whole = index[...]
    high = lax.div(whole, 32)
    low = whole - high * 32
    parts = [
        jnp.dot(
            chosen.astype(jnp.bfloat16),
            part.astype(jnp.float32).astype(jnp.bfloat16),
            preferred_element_type=jnp.float32,
        )
        for part in (high, low)
    ]
    of_member = (parts[0] * 32.0 + parts[1]).astype(jnp.int32)
    row = lax.broadcasted_iota(jnp.int32, (rows, RANK), 0)
    rank = lax.rem(first + lax.rem(row, period), RANK)
    column = lax.broadcasted_iota(jnp.int32, (rows, RANK), 1)
    return jnp.sum(jnp.where(column == rank, of_member, 0), axis=1, keepdims=True)


def one_hot(rows_of, rows):
    return (lax.broadcasted_iota(jnp.int32, (rows, BANK), 1) == rows_of).astype(jnp.float32)


def kernel(
    tokens, weight, a_bank, b_bank, index, mirror, rewards,
    hidden, update,
    tok, wts, acc, out, upd, banka, bankb, pick_a, pick_b, own_b, own_a, message, heard, low,
    w_got, w_sent, t_got, t_sent, m_got, m_sent, local,
):
    p = lax.axis_index("pop")
    f = lax.axis_index("fsdp")
    yl, z, c = p // 16, (p // 2) % Z, p % 2
    yh, x = f // X, f % X

    def pop_of(yl_, z_, c_):
        return yl_ * 16 + lax.rem(z_ + 2 * Z, Z) * 2 + c_

    def fsdp_of(yh_, x_):
        return yh_ * X + lax.rem(x_ + 2 * X, X)

    def sibling():
        return {"pop": pop_of(yl, z, 1 - c), "fsdp": f}

    def along_z(way):
        return {"pop": pop_of(yl, z + way, c), "fsdp": f}

    def across_y():
        return {"pop": pop_of(1 - yl, z, c), "fsdp": f}

    def along_x(way):
        return {"pop": p, "fsdp": fsdp_of(yh, x + way)}

    def far_y():
        return {"pop": p, "fsdp": fsdp_of(1 - yh, x)}

    barrier = pltpu.get_barrier_semaphore()

    def greet(j, _):
        peer = lax.rem(p + j, POP)
        pl.semaphore_signal(barrier, inc=1, device_id={"pop": peer, "fsdp": f}, device_id_type=MESH)
        return 0

    for way in (1, -1):
        pl.semaphore_signal(barrier, inc=1, device_id=along_x(way), device_id_type=MESH)
    pl.semaphore_signal(barrier, inc=1, device_id=far_y(), device_id_type=MESH)
    lax.fori_loop(1, POP, greet, 0)

    load_a = pltpu.make_async_copy(a_bank, banka, local.at[0])
    load_b = pltpu.make_async_copy(b_bank, bankb, local.at[1])
    load_t = pltpu.make_async_copy(tokens, tok.at[f], local.at[2])
    load_w = pltpu.make_async_copy(
        weight, wts.at[pl.ds(pl.multiple_of(p * 128, 128), 128)], local.at[3]
    )
    for copy in (load_a, load_w, load_t, load_b):
        copy.start()
    pl.semaphore_wait(barrier, POP - 1 + 3)

    sends = []

    def w_block(shard, half):
        return wts.at[pl.ds(pl.multiple_of(shard * 128 + half * 64, 64), 64)]

    def t_block(owner, half):
        return tok.at[owner, pl.ds(half * SEQ, SEQ)]

    counts = {"w": 0, "t": 0}

    def send_w(shard, half, target, own=False):
        k = counts["w"]
        counts["w"] += 1
        copy = pltpu.make_async_remote_copy(
            src_ref=weight.at[pl.ds(half * 64, 64)] if own else w_block(shard, half),
            dst_ref=w_block(shard, half),
            send_sem=w_sent.at[k],
            recv_sem=w_got.at[shard * 2 + half],
            device_id=target,
            device_id_type=MESH,
        )
        copy.start()
        sends.append(copy)

    def send_t(owner, half, target, own=False):
        k = counts["t"]
        counts["t"] += 1
        copy = pltpu.make_async_remote_copy(
            src_ref=tokens.at[pl.ds(half * SEQ, SEQ)] if own else t_block(owner, half),
            dst_ref=t_block(owner, half),
            send_sem=t_sent.at[k],
            recv_sem=t_got.at[owner * 2 + half],
            device_id=target,
            device_id_type=MESH,
        )
        copy.start()
        sends.append(copy)

    def wait_w(shard, half):
        block = w_block(shard, half)
        pltpu.make_async_copy(block, block, w_got.at[shard * 2 + half]).wait()

    def wait_t(owner, half):
        block = t_block(owner, half)
        pltpu.make_async_copy(block, block, t_got.at[owner * 2 + half]).wait()

    for half in (0, 1):
        for way in (1, -1):
            send_w(p, half, along_z(way), True)
        send_w(p, half, across_y(), True)
        for way in (1, -1):
            send_t(f, half, along_x(way), True)
        send_t(f, half, far_y(), True)
        send_w(p, half, sibling(), True)

    owed = [(pop_of(yl, z, 1 - c), 0), (pop_of(yl, z, 1 - c), 1)]

    def settle():
        for shard, half in owed:
            wait_w(shard, half)
        owed.clear()

    def got_own(d, way, half):
        z_ = z - way * d
        shard = pop_of(yl, z_, c)
        wait_w(shard, half)
        if d < 3 or (d == 3 and half == (0 if way == 1 else 1)):
            send_w(shard, half, along_z(way))
        send_w(shard, half, sibling())
        if (d == 3 and half == 1) or d == 4:
            send_w(shard, half, across_y())
        owed.append((pop_of(yl, z_, 1 - c), half))

    def got_other(d, way, half, forward=True):
        z_ = z - way * d
        shard = pop_of(1 - yl, z_, c)
        wait_w(shard, half)
        if forward and (d == 1 or (d == 2 and half == 0)):
            send_w(shard, half, along_z(way))
        send_w(shard, half, sibling())
        owed.append((pop_of(1 - yl, z_, 1 - c), half))

    def pass_other(half):
        for way in (1, -1):
            send_w(pop_of(1 - yl, z, c), half, along_z(way))

    def got_tokens(yh_, d, way, half):
        owner = fsdp_of(yh_, x - way * d)
        wait_t(owner, half)
        if d == 1 and half == (0 if way == 1 else 1):
            send_t(owner, half, along_x(way))

    def pass_tokens(half):
        for way in (1, -1):
            send_t(fsdp_of(1 - yh, x), half, along_x(way))

    load_a.wait()
    hot = one_hot(flat_rows(index, FACTORS, 0, FACTORS), FACTORS).astype(jnp.bfloat16)
    rows_a = picked(hot, banka[...])
    pick_a[...] = rows_a
    line = lax.broadcasted_iota(jnp.int32, (8, 128), 0)
    info = jnp.where(
        line == 0,
        rewards[0].astype(jnp.float32),
        jnp.where(
            line == 1,
            rewards[1].astype(jnp.float32),
            jnp.where(line == 2, mirror[0].astype(jnp.float32), mirror[1].astype(jnp.float32)),
        ),
    )
    message[...] = jnp.concatenate(
        [rows_a.reshape(POP, 8, 128), jnp.broadcast_to(info[None], (POP, 8, 128))], axis=1
    ).astype(jnp.bfloat16)

    def tell(j, _):
        peer = lax.rem(p + j, POP)
        pltpu.make_async_remote_copy(
            src_ref=message.at[peer],
            dst_ref=heard.at[p],
            send_sem=m_sent.at[j],
            recv_sem=m_got.at[p],
            device_id={"pop": peer, "fsdp": f},
            device_id_type=MESH,
        ).start()
        return 0

    lax.fori_loop(1, POP, tell, 0)
    heard[p] = message[p]

    for way in (1, -1):
        got_own(1, way, 0)

    load_b.wait()
    pick_b[...] = picked(hot, bankb[...]).astype(jnp.bfloat16)
    hot_own = one_hot(flat_rows(index, SLOT, p * 8, 8), SLOT)
    used = lax.broadcasted_iota(jnp.int32, (SLOT, BANK), 0) < 24
    own_b[...] = picked(jnp.where(used, hot_own, 0.0), bankb[...]).astype(jnp.bfloat16)
    acc[...] = jnp.zeros_like(acc)
    low[...] = jnp.zeros_like(low)

    for way in (1, -1):
        got_own(1, way, 1)

    def hear(j, _):
        peer = lax.rem(p + POP - j, POP)
        block = heard.at[peer]
        pltpu.make_async_copy(block, block, m_got.at[peer]).wait()
        return 0

    lax.fori_loop(1, POP, hear, 0)

    def lay(q, _):
        both = jnp.concatenate([heard[2 * q], heard[2 * q + 1]], axis=1).astype(jnp.float32)[:8]
        own_a[q] = jnp.concatenate(
            [both, both, both, jnp.zeros((SLOT - 24, TILE), jnp.float32)], axis=0
        ).astype(jnp.bfloat16)
        return 0

    lax.fori_loop(0, PIECES, lay, 0)

    told = heard[...].astype(jnp.float32)[:, 8:16, :].reshape(POP * 8, 128)
    row = lax.broadcasted_iota(jnp.int32, (FACTORS, POP * 8), 0)
    place = lax.broadcasted_iota(jnp.int32, (FACTORS, POP * 8), 1)
    member = lax.div(row, RANK)
    spot = lax.div(member, 2) * 8 + lax.rem(member, 2)
    told16 = told.astype(jnp.bfloat16)
    reward_of = picked((place == spot).astype(jnp.float32), told16)
    mirror_of = picked((place == spot + 2).astype(jnp.float32), told16)
    lane = lax.broadcasted_iota(jnp.int32, (POP * 8, 128), 1)
    at = lax.broadcasted_iota(jnp.int32, (POP * 8, 128), 0)
    mine = at == lax.div(lane, 2) * 8 + lax.rem(lane, 2)
    across = jnp.sum(jnp.where(mine, told, 0.0), axis=0, keepdims=True)
    lane = lax.broadcasted_iota(jnp.int32, (FACTORS, 128), 1)
    member = lax.div(lax.broadcasted_iota(jnp.int32, (FACTORS, 128), 0), RANK)
    ahead = (across < reward_of) | ((across == reward_of) & (lane < member))
    standing = jnp.sum(
        jnp.where(ahead & (lane < MEMBERS), 1.0, 0.0), axis=1, keepdims=True
    )
    coeff = (2.0 * standing - (MEMBERS - 1)) * (2.0 * mirror_of - 1.0)
    shaped = pick_a[...] * coeff
    high = shaped.astype(jnp.bfloat16)
    rest = (shaped - high.astype(jnp.float32)).astype(jnp.bfloat16)
    both = jnp.concatenate([high, rest], axis=0).astype(jnp.float32).T.astype(jnp.bfloat16)
    rows_b = pick_b[...]
    total = jnp.dot(
        both, jnp.concatenate([rows_b, rows_b], axis=0), preferred_element_type=jnp.float32
    )
    upd[...] = total * (1.0 / ((MEMBERS - 1) * math.sqrt(MEMBERS * RANK)))
    save_u = pltpu.make_async_copy(upd, update, local.at[4])
    save_u.start()

    def phase_of(q):
        x_, yl_, z_ = lax.rem(lax.div(q, 2), X), lax.div(q, Z), lax.rem(q, Z)
        dx = lax.rem(x_ - x + X, X)
        dz = lax.rem(z_ - z + Z, Z)
        dz = jnp.minimum(dz, Z - dz)
        near = jnp.where(dx == 2, 2, 1)
        far = jnp.where(dx == 0, 2, jnp.where(dx == 2, 6, 4))
        by_tokens = jnp.where(yl_ == yh, near, far)
        same = jnp.where(dz < 3, 1, 2)
        other = jnp.where(
            dz == 0, 1, jnp.where(dz == 1, 3, jnp.where(dz == 2, 5, jnp.where(dz == 3, 6, 4)))
        )
        by_weight = jnp.where(yl_ == yl, same, other)
        return jnp.maximum(by_tokens, by_weight)

    def work(q):
        lhs = tok[lax.div(q, 2), :, pl.ds(pl.multiple_of(lax.rem(q, 2) * TILE, TILE), TILE)]

        def tile(n, _):
            rhs = wts[
                pl.ds(pl.multiple_of(q * TILE, TILE), TILE),
                pl.ds(pl.multiple_of(n * TILE, TILE), TILE),
            ]
            acc[n] += jnp.dot(lhs, rhs, preferred_element_type=jnp.float32)
            return 0

        lax.fori_loop(0, TILES, tile, 0)
        low[...] += lax.dot_general(
            lhs, own_a[q], (((1,), (1,)), ((), ())), preferred_element_type=jnp.float32
        )

    def phase(number):
        settle()

        def step(q, _):
            @pl.when(phase_of(q) == number)
            def _():
                work(q)

            return 0

        lax.fori_loop(0, PIECES, step, 0)

    for way in (1, -1):
        got_own(2, way, 0)
    for way in (1, -1):
        got_tokens(yh, 1, way, 0)
    got_other(0, 1, 0)
    wait_t(fsdp_of(1 - yh, x), 0)
    pass_tokens(0)
    for way in (1, -1):
        got_own(2, way, 1)
    for way in (1, -1):
        got_tokens(yh, 1, way, 1)
    got_other(0, 1, 1)
    load_t.wait()
    load_w.wait()
    phase(1)
    for way in (1, -1):
        got_own(3, way, 0)
    pass_other(0)
    wait_t(fsdp_of(1 - yh, x), 1)
    pass_tokens(1)
    for way in (1, -1):
        got_own(3, way, 1)
    pass_other(1)
    got_tokens(yh, 2, 1, 0)
    got_tokens(yh, 2, -1, 1)
    got_own(4, 1, 0)
    got_own(4, -1, 1)
    phase(2)
    for half in (0, 1):
        for way in (1, -1):
            got_other(1, way, half)
    for way in (1, -1):
        got_other(3, way, 1, False)
    for way in (1, -1):
        got_tokens(1 - yh, 1, way, 0)
    phase(3)
    for way in (1, -1):
        got_other(2, way, 0)
    got_other(4, 1, 0)
    got_other(4, -1, 1)
    for way in (1, -1):
        got_tokens(1 - yh, 1, way, 1)
    phase(4)
    for way in (1, -1):
        got_other(2, way, 1)
    phase(5)
    for way in (1, -1):
        got_other(3, way, 0, False)
    got_tokens(1 - yh, 2, 1, 0)
    got_tokens(1 - yh, 2, -1, 1)
    phase(LAST)

    lane = lax.broadcasted_iota(jnp.int32, (ROWS, SLOT), 1)
    row = lax.broadcasted_iota(jnp.int32, (ROWS, SLOT), 0)
    own = lax.div(lax.rem(lane, 8), RANK) == lax.div(row, SEQ)
    signed = jnp.where(
        row < SEQ,
        (2 * mirror[0] - 1).astype(jnp.float32),
        (2 * mirror[1] - 1).astype(jnp.float32),
    )
    scaled = jnp.where(own, low[...] * (signed * (noise_scale / math.sqrt(D * RANK))), 0.0)
    first = scaled.astype(jnp.bfloat16).astype(jnp.float32)
    second = (scaled - first).astype(jnp.bfloat16).astype(jnp.float32)
    third = scaled - first - second
    parts = jnp.where(lane < 8, first, jnp.where(lane < 16, second, third)).astype(jnp.bfloat16)

    for n in range(TILES):
        columns = pl.ds(n * TILE, TILE)
        out[:, columns] = (
            acc[n] + jnp.dot(parts, own_b[:, columns], preferred_element_type=jnp.float32)
        ).astype(jnp.bfloat16)
        pltpu.make_async_copy(out.at[:, columns], hidden.at[:, columns], local.at[5 + n]).start()

    for copy in sends:
        copy.wait_send()

    def told_all(j, _):
        peer = lax.rem(p + j, POP)
        pltpu.make_async_copy(message.at[peer], message.at[peer], m_sent.at[j]).wait()
        return 0

    lax.fori_loop(1, POP, told_all, 0)
    save_u.wait()
    for n in range(TILES):
        columns = pl.ds(n * TILE, TILE)
        pltpu.make_async_copy(out.at[:, columns], hidden.at[:, columns], local.at[5 + n]).wait()


def per_device(tokens, up_weight, a_bank, b_bank, factor_index, mirror, rewards):
    any_space = pl.BlockSpec(memory_space=pl.ANY)
    smem = pl.BlockSpec(memory_space=pltpu.SMEM)
    dma = pltpu.SemaphoreType.DMA
    bf16, f32 = jnp.bfloat16, jnp.float32
    return pl.pallas_call(
        kernel,
        out_shape=(
            jax.ShapeDtypeStruct((ROWS, WIDTH), bf16),
            jax.ShapeDtypeStruct((128, WIDTH), f32),
        ),
        in_specs=[any_space] * 4 + [pl.BlockSpec(memory_space=pltpu.VMEM), smem, smem],
        out_specs=(any_space, any_space),
        scratch_shapes=[
            pltpu.VMEM((FSDP, ROWS, 512), bf16),
            pltpu.VMEM((D, WIDTH), bf16),
            pltpu.VMEM((TILES, ROWS, TILE), f32),
            pltpu.VMEM((ROWS, WIDTH), bf16),
            pltpu.VMEM((128, WIDTH), f32),
            pltpu.VMEM((BANK, 128), bf16),
            pltpu.VMEM((BANK, WIDTH), bf16),
            pltpu.VMEM((FACTORS, 128), f32),
            pltpu.VMEM((FACTORS, WIDTH), bf16),
            pltpu.VMEM((SLOT, WIDTH), bf16),
            pltpu.VMEM((PIECES, SLOT, TILE), bf16),
            pltpu.VMEM((POP, 16, 128), bf16),
            pltpu.VMEM((POP, 16, 128), bf16),
            pltpu.VMEM((ROWS, SLOT), f32),
            dma((64,)),
            dma((62,)),
            dma((16,)),
            dma((14,)),
            dma((POP,)),
            dma((POP,)),
            dma((5 + TILES,)),
        ],
        compiler_params=pltpu.CompilerParams(
            collective_id=1, has_side_effects=True, vmem_limit_bytes=56 * 2**20
        ),
        name="gather_project",
    )(tokens, up_weight, a_bank, b_bank, factor_index, mirror, rewards)


def solution(mesh):
    in_specs = (
        P("pop", "fsdp"),
        P("pop", "fsdp"),
        P(None, "pop"),
        P(None, "fsdp"),
        P(),
        P("pop"),
        P("pop"),
    )
    out_specs = (P("pop", "fsdp"), P("pop", "fsdp"))
    return jax.shard_map(
        per_device, mesh=mesh, in_specs=in_specs, out_specs=out_specs, check_vma=False
    )
```

time: 262 us -> 125 us (0.48)
  waiting for transfers between devices: 184 us -> 0 us
  Pallas kernels: 0 us -> 115 us
  matrix products: 29.2 us -> 0 us
  starting transfers between devices: 18.8 us -> 0 us
  between operations: 14.2 us -> 0.65 us
  local copies, waits for them, and re-layouts: 12.7 us -> 6.19 us
    all_gather x2 -> x0, waiting for transfers between devices: 130 us -> none  [the longest x1 87.2 us: per_device(): entire_weight = lax.all_gather(up_weight, 'pop', axis=0, tiled=True)]
    pallas_call x0 -> x1, Pallas kernels: none -> 115 us  [per_device(): pl.pallas_call(kernel, out_shape=(jax.ShapeDtypeStruct((ROWS, WIDTH), bf1...]
    all_to_all x3 -> x0, waiting for transfers between devices: 52.2 us -> none  [sent_to_all(): return lax.all_to_all(copies, axis, split_axis=0, concat_axis=0, tiled=True)]
    dot_general x4 -> x0, matrix products: 29.2 us -> none  [the longest x1 17 us: per_device(): jnp.dot(piece, entire_weight, preferred_element_type=jnp.float32)]
    all_to_all x3 -> x0, starting transfers between devices: 18.8 us -> none  [sent_to_all(): return lax.all_to_all(copies, axis, split_axis=0, concat_axis=0, tiled=True)]
    gather x2 -> x0, local copies, waits for them, and re-layouts: 6.44 us -> none  [the longest x1 5.58 us: per_device(): picked_b = jnp.take(b_bank, flat_index, axis=0)]
    unnamed x5, local copies, waits for them, and re-layouts: 0.79 us -> 6.19 us
    broadcast_in_dim x5 -> x0, local copies, waits for them, and re-layouts: 4.24 us -> none  [the longest x3 4.1 us: sent_to_all(): copies = jnp.broadcast_to(array, (lax.axis_size(axis), *array.shape))]
  transfers between devices with their start and end apart: 5 -> 0, of which waited for: 5 -> 0; matrix products, arithmetic and copies ran while one was open for 9% -> 0% of each run, Pallas kernels for 0% -> 0%
where the time goes in v1:
time: 125 us; the launch traced here: 122 us
  Pallas kernels  115 us (92%)
  local copies, waits for them, and re-layouts  6.19 us (5%)
    pallas_call x1, Pallas kernels, per_device(): pl.pallas_call(kernel, out_shape=(jax.ShapeDtypeStruct((ROWS, WIDTH), bf1...  115 us
    unnamed x5, local copies, waits for them, and re-layouts  6.19 us

profile of v1, /device:TPU:17, one launch (start us, length us, event | category | flops | bytes accessed | tf_op | source)
XLA Modules:
  0.0 122.3 jit_solution(462320647214701437)
XLA Ops:
  0.6 1.4 %copy.9.index = s32[64,4]{1,0:T(8,128)} copy(s32[64,4]{0,1:T(4,128)} %param.11) | data formatting | bytes 2048 | tf_op args[4]
  2.0 115.4 %gather_project.1 = (bf16[896,1792]{1,0:T(8,128)(2,1)}, f32[128,1792]{1,0:T(8,128)}) custom-call(bf16[896,512]{1,0:T(8,128)(2,1)} %tokens.1, bf16[128,1792]{1,0:T(8,128)(2,1)} %weight.1, bf16[1024,128]{1,0:T(8,128)(2,1)} %a_bank.1, bf16[1024,1792]{1,0:T(8,128)(2,1)} %b_bank.1, s32[64,4]{1,0:T(8,128)} %copy.9.index, s32[2]{0:T(128)} %mirror.1, s32[2]{0:T(128)} %rewards.1), custom_call_target="tpu_custom_call" | custom-call | tf_op jit(solution)/shard_map/gather_project/pallas_call | solution.py:441
  117.5 0.0 copy-start
  117.5 3.9 %copy.12 = bf16[896,1792]{1,0:T(8,128)(2,1)} copy(bf16[896,1792]{1,0:T(8,128)(2,1)} %get-tuple-element.4) | data formatting | bytes 6422528
  121.4 0.0 copy-done
  121.4 0.9 copy.13
Async XLA Ops:
  117.5 3.9 %copy-start = (f32[128,1792]{1,0:T(8,128)S(1)}, f32[128,1792]{1,0:T(8,128)}, u32[]{:S(2)}) copy-start(f32[128,1792]{1,0:T(8,128)} %get-tuple-element.5) | copy-start | bytes 2752516

commit v2 on v1

--- a/solution.py
+++ b/solution.py
@@ -39,9 +39,10 @@
     high = lax.div(whole, 32)
     low = whole - high * 32
     parts = [
-        jnp.dot(
+        lax.dot_general(
             chosen.astype(jnp.bfloat16),
             part.astype(jnp.float32).astype(jnp.bfloat16),
+            (((1,), (1,)), ((), ())),
             preferred_element_type=jnp.float32,
         )
         for part in (high, low)
@@ -60,7 +61,7 @@
 def kernel(
     tokens, weight, a_bank, b_bank, index, mirror, rewards,
     hidden, update,
-    tok, wts, acc, out, upd, banka, bankb, pick_a, pick_b, own_b, own_a, message, heard, low,
+    tok, wts, acc, banka, bankb, pick_a, pick_b, own_b, own_a, message, heard, low,
     w_got, w_sent, t_got, t_sent, m_got, m_sent, local,
 ):
     p = lax.axis_index("pop")
@@ -109,6 +110,26 @@
     )
     for copy in (load_a, load_w, load_t, load_b):
         copy.start()
+
+    load_a.wait()
+    hot = one_hot(flat_rows(index, FACTORS, 0, FACTORS), FACTORS).astype(jnp.bfloat16)
+    rows_a = picked(hot, banka[...])
+    pick_a[...] = rows_a
+    line = lax.broadcasted_iota(jnp.int32, (8, 128), 0)
+    info = jnp.where(
+        line == 0,
+        rewards[0].astype(jnp.float32),
+        jnp.where(
+            line == 1,
+            rewards[1].astype(jnp.float32),
+            jnp.where(line == 2, mirror[0].astype(jnp.float32), mirror[1].astype(jnp.float32)),
+        ),
+    )
+    message[...] = jnp.concatenate(
+        [rows_a.reshape(POP, 8, 128), jnp.broadcast_to(info[None], (POP, 8, 128))], axis=1
+    ).astype(jnp.bfloat16)
+
+    heard[p] = message[p]
     pl.semaphore_wait(barrier, POP - 1 + 3)
 
     sends = []
@@ -157,14 +178,54 @@
         block = t_block(owner, half)
         pltpu.make_async_copy(block, block, t_got.at[owner * 2 + half]).wait()
 
-    for half in (0, 1):
-        for way in (1, -1):
-            send_w(p, half, along_z(way), True)
-        send_w(p, half, across_y(), True)
-        for way in (1, -1):
-            send_t(f, half, along_x(way), True)
-        send_t(f, half, far_y(), True)
-        send_w(p, half, sibling(), True)
+    for turn in (0, 1):
+        for way in (1, -1):
+            send_w(p, turn if way == 1 else 1 - turn, along_z(way), True)
+        for way in (1, -1):
+            send_t(f, turn if way == 1 else 1 - turn, along_x(way), True)
+        if turn == 0:
+            def tell(j, _):
+                peer = lax.rem(p + j, POP)
+                pltpu.make_async_remote_copy(
+                    src_ref=message.at[peer],
+                    dst_ref=heard.at[p],
+                    send_sem=m_sent.at[j],
+                    recv_sem=m_got.at[p],
+                    device_id={"pop": peer, "fsdp": f},
+                    device_id_type=MESH,
+                ).start()
+                return 0
+
+            lax.fori_loop(1, POP, tell, 0)
+        send_t(f, turn, far_y(), True)
+        send_w(p, turn, across_y(), True)
+        send_w(p, turn, sibling(), True)
+
+    def phase_of(q):
+        x_, yl_, z_ = (q // 2) % X, q // Z, q % Z
+        dx = lax.rem(x_ - x + X, X)
+        dz = lax.rem(z_ - z + Z, Z)
+        dz = jnp.minimum(dz, Z - dz)
+        near = jnp.where(dx == 2, 2, 1)
+        far = jnp.where(dx == 0, 2, jnp.where(dx == 2, 6, 4))
+        by_tokens = jnp.where(yl_ == yh, near, far)
+        same = jnp.where(dz < 3, 1, 2)
+        other = jnp.where(
+            dz == 0, 1, jnp.where(dz == 1, 3, jnp.where(dz == 2, 5, jnp.where(dz == 3, 6, 4)))
+        )
+        by_weight = jnp.where(yl_ == yl, same, other)
+        return jnp.maximum(by_tokens, by_weight)
+
+
+    keys = [phase_of(q) * PIECES + q for q in range(PIECES)]
+    places = [sum((other < key).astype(jnp.int32) for other in keys if other is not key) for key in keys]
+    ends = [
+        sum((key < (number + 1) * PIECES).astype(jnp.int32) for key in keys)
+        for number in range(LAST + 1)
+    ]
+
+    def piece_at(k):
+        return sum(jnp.where(place == k, q, 0) for q, place in enumerate(places))
 
     owed = [(pop_of(yl, z, 1 - c), 0), (pop_of(yl, z, 1 - c), 1)]
 
@@ -203,56 +264,58 @@
         if d == 1 and half == (0 if way == 1 else 1):
             send_t(owner, half, along_x(way))
 
-    def pass_tokens(half):
-        for way in (1, -1):
-            send_t(fsdp_of(1 - yh, x), half, along_x(way))
-
-    load_a.wait()
-    hot = one_hot(flat_rows(index, FACTORS, 0, FACTORS), FACTORS).astype(jnp.bfloat16)
-    rows_a = picked(hot, banka[...])
-    pick_a[...] = rows_a
-    line = lax.broadcasted_iota(jnp.int32, (8, 128), 0)
-    info = jnp.where(
-        line == 0,
-        rewards[0].astype(jnp.float32),
-        jnp.where(
-            line == 1,
-            rewards[1].astype(jnp.float32),
-            jnp.where(line == 2, mirror[0].astype(jnp.float32), mirror[1].astype(jnp.float32)),
-        ),
-    )
-    message[...] = jnp.concatenate(
-        [rows_a.reshape(POP, 8, 128), jnp.broadcast_to(info[None], (POP, 8, 128))], axis=1
-    ).astype(jnp.bfloat16)
-
-    def tell(j, _):
-        peer = lax.rem(p + j, POP)
-        pltpu.make_async_remote_copy(
-            src_ref=message.at[peer],
-            dst_ref=heard.at[p],
-            send_sem=m_sent.at[j],
-            recv_sem=m_got.at[p],
-            device_id={"pop": peer, "fsdp": f},
-            device_id_type=MESH,
-        ).start()
-        return 0
-
-    lax.fori_loop(1, POP, tell, 0)
-    heard[p] = message[p]
-
-    for way in (1, -1):
-        got_own(1, way, 0)
-
+    def pass_tokens(turn):
+        for way in (1, -1):
+            send_t(fsdp_of(1 - yh, x), turn if way == 1 else 1 - turn, along_x(way))
+
+    def work(q):
+        lhs = tok[lax.div(q, 2), :, pl.ds(pl.multiple_of(lax.rem(q, 2) * TILE, TILE), TILE)]
+        features = pl.ds(pl.multiple_of(q * TILE, TILE), TILE)
+        for n in range(TILES):
+            acc[n] += jnp.dot(
+                lhs, wts[features, n * TILE : (n + 1) * TILE], preferred_element_type=jnp.float32
+            )
+        low[...] += jnp.dot(lhs, own_a[q], preferred_element_type=jnp.float32)
+
+    done = [0]
+
+    def multiply(number, most):
+        stop = jnp.minimum(done[0] + most, ends[number])
+
+        def step(k, _):
+            work(piece_at(k))
+            return 0
+
+        lax.fori_loop(done[0], stop, step, 0)
+        done[0] = stop
+
+    def own_turn(d, turn):
+        for way in (1, -1):
+            got_own(d, way, turn if way == 1 else 1 - turn)
+
+    def other_turn(d, half, forward=True):
+        for way in (1, -1):
+            got_other(d, way, half, forward)
+
+    def token_turn(yh_, turn):
+        for way in (1, -1):
+            got_tokens(yh_, 1, way, turn if way == 1 else 1 - turn)
+
+    own_turn(1, 0)
     load_b.wait()
     pick_b[...] = picked(hot, bankb[...]).astype(jnp.bfloat16)
+    own_turn(1, 1)
+    token_turn(yh, 0)
     hot_own = one_hot(flat_rows(index, SLOT, p * 8, 8), SLOT)
     used = lax.broadcasted_iota(jnp.int32, (SLOT, BANK), 0) < 24
     own_b[...] = picked(jnp.where(used, hot_own, 0.0), bankb[...]).astype(jnp.bfloat16)
+    own_turn(2, 0)
     acc[...] = jnp.zeros_like(acc)
     low[...] = jnp.zeros_like(low)
-
-    for way in (1, -1):
-        got_own(1, way, 1)
+    load_t.wait()
+    load_w.wait()
+    own_turn(2, 1)
+    token_turn(yh, 1)
 
     def hear(j, _):
         peer = lax.rem(p + POP - j, POP)
@@ -266,11 +329,28 @@
         both = jnp.concatenate([heard[2 * q], heard[2 * q + 1]], axis=1).astype(jnp.float32)[:8]
         own_a[q] = jnp.concatenate(
             [both, both, both, jnp.zeros((SLOT - 24, TILE), jnp.float32)], axis=0
-        ).astype(jnp.bfloat16)
+        ).T.astype(jnp.bfloat16)
         return 0
 
     lax.fori_loop(0, PIECES, lay, 0)
 
+    for half in (0, 1):
+        got_other(0, 1, half)
+    own_turn(3, 0)
+    settle()
+    multiply(1, 2)
+    wait_t(fsdp_of(1 - yh, x), 0)
+    wait_t(fsdp_of(1 - yh, x), 1)
+    for turn in (0, 1):
+        pass_tokens(turn)
+    own_turn(3, 1)
+    pass_other(0)
+    pass_other(1)
+    got_tokens(yh, 2, 1, 0)
+    got_tokens(yh, 2, -1, 1)
+    multiply(1, 3)
+    got_own(4, 1, 0)
+    got_own(4, -1, 1)
     told = heard[...].astype(jnp.float32)[:, 8:16, :].reshape(POP * 8, 128)
     row = lax.broadcasted_iota(jnp.int32, (FACTORS, POP * 8), 0)
     place = lax.broadcasted_iota(jnp.int32, (FACTORS, POP * 8), 1)
@@ -298,104 +378,31 @@
     total = jnp.dot(
         both, jnp.concatenate([rows_b, rows_b], axis=0), preferred_element_type=jnp.float32
     )
-    upd[...] = total * (1.0 / ((MEMBERS - 1) * math.sqrt(MEMBERS * RANK)))
-    save_u = pltpu.make_async_copy(upd, update, local.at[4])
-    save_u.start()
-
-    def phase_of(q):
-        x_, yl_, z_ = lax.rem(lax.div(q, 2), X), lax.div(q, Z), lax.rem(q, Z)
-        dx = lax.rem(x_ - x + X, X)
-        dz = lax.rem(z_ - z + Z, Z)
-        dz = jnp.minimum(dz, Z - dz)
-        near = jnp.where(dx == 2, 2, 1)
-        far = jnp.where(dx == 0, 2, jnp.where(dx == 2, 6, 4))
-        by_tokens = jnp.where(yl_ == yh, near, far)
-        same = jnp.where(dz < 3, 1, 2)
-        other = jnp.where(
-            dz == 0, 1, jnp.where(dz == 1, 3, jnp.where(dz == 2, 5, jnp.where(dz == 3, 6, 4)))
-        )
-        by_weight = jnp.where(yl_ == yl, same, other)
-        return jnp.maximum(by_tokens, by_weight)
-
-    def work(q):
-        lhs = tok[lax.div(q, 2), :, pl.ds(pl.multiple_of(lax.rem(q, 2) * TILE, TILE), TILE)]
-
-        def tile(n, _):
-            rhs = wts[
-                pl.ds(pl.multiple_of(q * TILE, TILE), TILE),
-                pl.ds(pl.multiple_of(n * TILE, TILE), TILE),
-            ]
-            acc[n] += jnp.dot(lhs, rhs, preferred_element_type=jnp.float32)
-            return 0
-
-        lax.fori_loop(0, TILES, tile, 0)
-        low[...] += lax.dot_general(
-            lhs, own_a[q], (((1,), (1,)), ((), ())), preferred_element_type=jnp.float32
-        )
-
-    def phase(number):
-        settle()
-
-        def step(q, _):
-            @pl.when(phase_of(q) == number)
-            def _():
-                work(q)
-
-            return 0
-
-        lax.fori_loop(0, PIECES, step, 0)
-
-    for way in (1, -1):
-        got_own(2, way, 0)
-    for way in (1, -1):
-        got_tokens(yh, 1, way, 0)
-    got_other(0, 1, 0)
-    wait_t(fsdp_of(1 - yh, x), 0)
-    pass_tokens(0)
-    for way in (1, -1):
-        got_own(2, way, 1)
-    for way in (1, -1):
-        got_tokens(yh, 1, way, 1)
-    got_other(0, 1, 1)
-    load_t.wait()
-    load_w.wait()
-    phase(1)
-    for way in (1, -1):
-        got_own(3, way, 0)
-    pass_other(0)
-    wait_t(fsdp_of(1 - yh, x), 1)
-    pass_tokens(1)
-    for way in (1, -1):
-        got_own(3, way, 1)
-    pass_other(1)
-    got_tokens(yh, 2, 1, 0)
-    got_tokens(yh, 2, -1, 1)
-    got_own(4, 1, 0)
-    got_own(4, -1, 1)
-    phase(2)
-    for half in (0, 1):
-        for way in (1, -1):
-            got_other(1, way, half)
-    for way in (1, -1):
-        got_other(3, way, 1, False)
-    for way in (1, -1):
-        got_tokens(1 - yh, 1, way, 0)
-    phase(3)
-    for way in (1, -1):
-        got_other(2, way, 0)
+    update[...] = total * (1.0 / ((MEMBERS - 1) * math.sqrt(MEMBERS * RANK)))
+
+    settle()
+    multiply(2, 2)
+    other_turn(1, 0)
+    token_turn(1 - yh, 0)
+    multiply(2, 3)
+    other_turn(1, 1)
+    other_turn(3, 1, False)
+    settle()
+    multiply(3, 3)
+    other_turn(2, 0)
     got_other(4, 1, 0)
     got_other(4, -1, 1)
-    for way in (1, -1):
-        got_tokens(1 - yh, 1, way, 1)
-    phase(4)
-    for way in (1, -1):
-        got_other(2, way, 1)
-    phase(5)
-    for way in (1, -1):
-        got_other(3, way, 0, False)
+    token_turn(1 - yh, 1)
+    settle()
+    multiply(4, 3)
+    other_turn(2, 1)
+    settle()
+    multiply(5, PIECES)
+    other_turn(3, 0, False)
+    settle()
     got_tokens(1 - yh, 2, 1, 0)
     got_tokens(1 - yh, 2, -1, 1)
-    phase(LAST)
+    multiply(LAST, PIECES)
 
     lane = lax.broadcasted_iota(jnp.int32, (ROWS, SLOT), 1)
     row = lax.broadcasted_iota(jnp.int32, (ROWS, SLOT), 0)
@@ -413,10 +420,9 @@
 
     for n in range(TILES):
         columns = pl.ds(n * TILE, TILE)
-        out[:, columns] = (
+        hidden[:, columns] = (
             acc[n] + jnp.dot(parts, own_b[:, columns], preferred_element_type=jnp.float32)
         ).astype(jnp.bfloat16)
-        pltpu.make_async_copy(out.at[:, columns], hidden.at[:, columns], local.at[5 + n]).start()
 
     for copy in sends:
         copy.wait_send()
@@ -427,10 +433,6 @@
         return 0
 
     lax.fori_loop(1, POP, told_all, 0)
-    save_u.wait()
-    for n in range(TILES):
-        columns = pl.ds(n * TILE, TILE)
-        pltpu.make_async_copy(out.at[:, columns], hidden.at[:, columns], local.at[5 + n]).wait()
 
 
 def per_device(tokens, up_weight, a_bank, b_bank, factor_index, mirror, rewards):
@@ -440,24 +442,19 @@
     bf16, f32 = jnp.bfloat16, jnp.float32
     return pl.pallas_call(
         kernel,
-        out_shape=(
-            jax.ShapeDtypeStruct((ROWS, WIDTH), bf16),
-            jax.ShapeDtypeStruct((128, WIDTH), f32),
-        ),
+        out_shape=(pltpu.VMEM((ROWS, WIDTH), bf16), pltpu.VMEM((128, WIDTH), f32)),
         in_specs=[any_space] * 4 + [pl.BlockSpec(memory_space=pltpu.VMEM), smem, smem],
-        out_specs=(any_space, any_space),
+        out_specs=(pl.BlockSpec(memory_space=pltpu.VMEM),) * 2,
         scratch_shapes=[
             pltpu.VMEM((FSDP, ROWS, 512), bf16),
             pltpu.VMEM((D, WIDTH), bf16),
             pltpu.VMEM((TILES, ROWS, TILE), f32),
-            pltpu.VMEM((ROWS, WIDTH), bf16),
-            pltpu.VMEM((128, WIDTH), f32),
             pltpu.VMEM((BANK, 128), bf16),
             pltpu.VMEM((BANK, WIDTH), bf16),
             pltpu.VMEM((FACTORS, 128), f32),
             pltpu.VMEM((FACTORS, WIDTH), bf16),
             pltpu.VMEM((SLOT, WIDTH), bf16),
-            pltpu.VMEM((PIECES, SLOT, TILE), bf16),
+            pltpu.VMEM((PIECES, TILE, SLOT), bf16),
             pltpu.VMEM((POP, 16, 128), bf16),
             pltpu.VMEM((POP, 16, 128), bf16),
             pltpu.VMEM((ROWS, SLOT), f32),
@@ -467,13 +464,13 @@
             dma((14,)),
             dma((POP,)),
             dma((POP,)),
-            dma((5 + TILES,)),
+            dma((4,)),
         ],
         compiler_params=pltpu.CompilerParams(
             collective_id=1, has_side_effects=True, vmem_limit_bytes=56 * 2**20
         ),
         name="gather_project",
-    )(tokens, up_weight, a_bank, b_bank, factor_index, mirror, rewards)
+    )(tokens, up_weight, a_bank, b_bank, factor_index.T, mirror, rewards)
 
 
 def solution(mesh):

time: 125 us -> 91.8 us (0.73); the launches traced: 122 us -> 91.7 us
  Pallas kernels: 115 us -> 88.4 us
  local copies, waits for them, and re-layouts: 6.19 us -> 2.61 us
    pallas_call x1, Pallas kernels: 115 us -> 88.4 us  [per_device(): pl.pallas_call(kernel, out_shape=(pltpu.VMEM((ROWS, WIDTH), bf16), pltpu....]
    unnamed x5 -> x2, local copies, waits for them, and re-layouts: 6.19 us -> 2.61 us
where the time goes in v2:
time: 91.8 us; the launch traced here: 91.7 us
  Pallas kernels  88.4 us (96%)
  local copies, waits for them, and re-layouts  2.61 us (3%)
    pallas_call x1, Pallas kernels, per_device(): pl.pallas_call(kernel, out_shape=(pltpu.VMEM((ROWS, WIDTH), bf16), pltpu....  88.4 us
    unnamed x2, local copies, waits for them, and re-layouts  2.61 us

profile of v2, /device:TPU:17, one launch (start us, length us, event | category | flops | bytes accessed | tf_op | source)
XLA Modules:
  0.0 91.7 jit_solution(2807248086969691400)
XLA Ops:
  0.6 88.4 %gather_project.1 = (bf16[896,1792]{1,0:T(8,128)(2,1)S(1)}, f32[128,1792]{1,0:T(8,128)S(1)}) custom-call(bf16[896,512]{1,0:T(8,128)(2,1)} %tokens.1, bf16[128,1792]{1,0:T(8,128)(2,1)} %weight.1, bf16[1024,128]{1,0:T(8,128)(2,1)} %a_bank.1, bf16[1024,1792]{1,0:T(8,128)(2,1)} %b_bank.1, s32[4,64]{1,0:T(4,128)} %bitcast.1, s32[2]{0:T(128)} %mirror.1, s32[2]{0:T(128)} %rewards.1), custom_call_target="tpu_custom_call" | custom-call | tf_op jit(solution)/shard_map/gather_project/pallas_call | solution.py:443
  89.1 1.7 %copy.11 = bf16[896,1792]{1,0:T(8,128)(2,1)} copy(bf16[896,1792]{1,0:T(8,128)(2,1)S(1)} %get-tuple-element.2) | data formatting | bytes 6422528
  90.8 0.9 %copy.12 = f32[128,1792]{1,0:T(8,128)} copy(f32[128,1792]{1,0:T(8,128)S(1)} %get-tuple-element.3) | data formatting | bytes 1835008

commit v3 on v2

--- a/solution.py
+++ b/solution.py
@@ -60,8 +60,8 @@
 
 def kernel(
     tokens, weight, a_bank, b_bank, index, mirror, rewards,
-    hidden, update,
-    tok, wts, acc, banka, bankb, pick_a, pick_b, own_b, own_a, message, heard, low,
+    acc, low, own_b, update,
+    tok, wts, banka, bankb, pick_a, pick_b, own_a, message, heard,
     w_got, w_sent, t_got, t_sent, m_got, m_sent, local,
 ):
     p = lax.axis_index("pop")
@@ -394,7 +394,7 @@
     got_other(4, -1, 1)
     token_turn(1 - yh, 1)
     settle()
-    multiply(4, 3)
+    multiply(4, 5)
     other_turn(2, 1)
     settle()
     multiply(5, PIECES)
@@ -404,6 +404,20 @@
     got_tokens(1 - yh, 2, -1, 1)
     multiply(LAST, PIECES)
 
+    for copy in sends:
+        copy.wait_send()
+
+    def told_all(j, _):
+        peer = lax.rem(p + j, POP)
+        pltpu.make_async_copy(message.at[peer], message.at[peer], m_sent.at[j]).wait()
+        return 0
+
+    lax.fori_loop(1, POP, told_all, 0)
+
+
+def finish(acc, low, own_b, shaped, mirror, hidden, update, out, done):
+    save = pltpu.make_async_copy(shaped, update, done.at[TILES])
+    save.start()
     lane = lax.broadcasted_iota(jnp.int32, (ROWS, SLOT), 1)
     row = lax.broadcasted_iota(jnp.int32, (ROWS, SLOT), 0)
     own = lax.div(lax.rem(lane, 8), RANK) == lax.div(row, SEQ)
@@ -418,46 +432,44 @@
     third = scaled - first - second
     parts = jnp.where(lane < 8, first, jnp.where(lane < 16, second, third)).astype(jnp.bfloat16)
 
+    saves = [save]
     for n in range(TILES):
         columns = pl.ds(n * TILE, TILE)
-        hidden[:, columns] = (
+        out[:, columns] = (
             acc[n] + jnp.dot(parts, own_b[:, columns], preferred_element_type=jnp.float32)
         ).astype(jnp.bfloat16)
-
-    for copy in sends:
-        copy.wait_send()
-
-    def told_all(j, _):
-        peer = lax.rem(p + j, POP)
-        pltpu.make_async_copy(message.at[peer], message.at[peer], m_sent.at[j]).wait()
-        return 0
-
-    lax.fori_loop(1, POP, told_all, 0)
+        saves.append(pltpu.make_async_copy(out.at[:, columns], hidden.at[:, columns], done.at[n]))
+        saves[-1].start()
+    for save in saves:
+        save.wait()
 
 
 def per_device(tokens, up_weight, a_bank, b_bank, factor_index, mirror, rewards):
     any_space = pl.BlockSpec(memory_space=pl.ANY)
     smem = pl.BlockSpec(memory_space=pltpu.SMEM)
+    vmem = pl.BlockSpec(memory_space=pltpu.VMEM)
     dma = pltpu.SemaphoreType.DMA
     bf16, f32 = jnp.bfloat16, jnp.float32
-    return pl.pallas_call(
+    acc, low, own_b, shaped = pl.pallas_call(
         kernel,
-        out_shape=(pltpu.VMEM((ROWS, WIDTH), bf16), pltpu.VMEM((128, WIDTH), f32)),
-        in_specs=[any_space] * 4 + [pl.BlockSpec(memory_space=pltpu.VMEM), smem, smem],
-        out_specs=(pl.BlockSpec(memory_space=pltpu.VMEM),) * 2,
+        out_shape=(
+            pltpu.VMEM((TILES, ROWS, TILE), f32),
+            pltpu.VMEM((ROWS, SLOT), f32),
+            pltpu.VMEM((SLOT, WIDTH), bf16),
+            pltpu.VMEM((128, WIDTH), f32),
+        ),
+        in_specs=[any_space] * 4 + [vmem, smem, smem],
+        out_specs=(vmem,) * 4,
         scratch_shapes=[
             pltpu.VMEM((FSDP, ROWS, 512), bf16),
             pltpu.VMEM((D, WIDTH), bf16),
-            pltpu.VMEM((TILES, ROWS, TILE), f32),
             pltpu.VMEM((BANK, 128), bf16),
             pltpu.VMEM((BANK, WIDTH), bf16),
             pltpu.VMEM((FACTORS, 128), f32),
             pltpu.VMEM((FACTORS, WIDTH), bf16),
-            pltpu.VMEM((SLOT, WIDTH), bf16),
             pltpu.VMEM((PIECES, TILE, SLOT), bf16),
             pltpu.VMEM((POP, 16, 128), bf16),
             pltpu.VMEM((POP, 16, 128), bf16),
-            pltpu.VMEM((ROWS, SLOT), f32),
             dma((64,)),
             dma((62,)),
             dma((16,)),
@@ -467,10 +479,26 @@
             dma((4,)),
         ],
         compiler_params=pltpu.CompilerParams(
-            collective_id=1, has_side_effects=True, vmem_limit_bytes=56 * 2**20
+            collective_id=1, has_side_effects=True, vmem_limit_bytes=55 * 2**20
         ),
         name="gather_project",
     )(tokens, up_weight, a_bank, b_bank, factor_index.T, mirror, rewards)
+    held = [
+        pltpu.with_memory_space_constraint(array, pltpu.VMEM)
+        for array in (acc, low, own_b, shaped)
+    ]
+    return pl.pallas_call(
+        finish,
+        out_shape=(
+            jax.ShapeDtypeStruct((ROWS, WIDTH), bf16),
+            jax.ShapeDtypeStruct((128, WIDTH), f32),
+        ),
+        in_specs=[vmem] * 4 + [smem],
+        out_specs=(any_space, any_space),
+        scratch_shapes=[pltpu.VMEM((ROWS, WIDTH), bf16), dma((TILES + 1,))],
+        compiler_params=pltpu.CompilerParams(vmem_limit_bytes=16 * 2**20),
+        name="finish",
+    )(*held, mirror)
 
 
 def solution(mesh):

time: 91.8 us -> 91 us (level)
  local copies, waits for them, and re-layouts: 2.61 us -> 0.01 us
  Pallas kernels: 88.4 us -> 90.1 us
    unnamed x2, local copies, waits for them, and re-layouts: 2.61 us -> 0.01 us
    pallas_call x1 -> x2, Pallas kernels: 88.4 us -> 90.1 us  [the longest x1 87.3 us: per_device(): pl.pallas_call(kernel, out_shape=(pltpu.VMEM((TILES, ROWS, TILE), f32), p...]
where the time goes in v3:
time: 91 us; the launch traced here: 90.9 us
  Pallas kernels  90.1 us (99%)
    pallas_call x1, Pallas kernels, per_device(): pl.pallas_call(kernel, out_shape=(pltpu.VMEM((TILES, ROWS, TILE), f32), p...  87.3 us
    pallas_call x1, Pallas kernels, per_device(): pl.pallas_call(finish, out_shape=(jax.ShapeDtypeStruct((ROWS, WIDTH), bf1...  2.8 us

profile of v3, /device:TPU:17, one launch (start us, length us, event | category | flops | bytes accessed | tf_op | source)
XLA Modules:
  0.0 90.9 jit_solution(15350941729072110866)
XLA Ops:
  0.6 0.0 copy-start
  0.6 87.3 %gather_project.1 = (f32[7,896,256]{2,1,0:T(8,128)S(1)}, f32[896,128]{1,0:T(8,128)S(1)}, bf16[128,1792]{1,0:T(8,128)(2,1)S(1)}, f32[128,1792]{1,0:T(8,128)S(1)}) custom-call(bf16[896,512]{1,0:T(8,128)(2,1)} %tokens.1, bf16[128,1792]{1,0:T(8,128)(2,1)} %weight.1, bf16[1024,128]{1,0:T(8,128)(2,1)} %a_bank.1, bf16[1024,1792]{1,0:T(8,128)(2,1)} %b_bank.1, ...), custom_call_target="tpu_custom_call" | custom-call | tf_op jit(solution)/shard_map/gather_project/pallas_call | solution.py:453
  87.9 0.0 copy-done
  88.0 2.8 %finish.1 = (bf16[896,1792]{1,0:T(8,128)(2,1)}, f32[128,1792]{1,0:T(8,128)}) custom-call(f32[7,896,256]{2,1,0:T(8,128)S(1)} %get-tuple-element.6.acc, f32[896,128]{1,0:T(8,128)S(1)} %get-tuple-element.7.low, bf16[128,1792]{1,0:T(8,128)(2,1)S(1)} %get-tuple-element.8.own_b, f32[128,1792]{1,0:T(8,128)S(1)} %get-tuple-element.9.shaped, s32[2]{0:T(128)S(1)} %copy-done), custom_call_target="tpu_custom_call" | custom-call | tf_op jit(solution)/shard_map/finish/pallas_call | solution.py:490
Async XLA Ops:
  0.6 87.3 %copy-start = (s32[2]{0:T(128)S(1)}, s32[2]{0:T(128)}, u32[]{:S(2)}) copy-start(s32[2]{0:T(128)} %mirror.3) | copy-start | bytes 28

commit v4 on v3

--- a/solution.py
+++ b/solution.py
@@ -397,8 +397,9 @@
     multiply(4, 5)
     other_turn(2, 1)
     settle()
+    multiply(5, 3)
+    other_turn(3, 0, False)
     multiply(5, PIECES)
-    other_turn(3, 0, False)
     settle()
     got_tokens(1 - yh, 2, 1, 0)
     got_tokens(1 - yh, 2, -1, 1)

time: 91 us -> 91 us (level)
  no operation moved by 1% of the time
where the time goes in v4:
time: 91 us; the launch traced here: 90.9 us
  Pallas kernels  90.1 us (99%)
    pallas_call x1, Pallas kernels, per_device(): pl.pallas_call(kernel, out_shape=(pltpu.VMEM((TILES, ROWS, TILE), f32), p...  87.3 us
    pallas_call x1, Pallas kernels, per_device(): pl.pallas_call(finish, out_shape=(jax.ShapeDtypeStruct((ROWS, WIDTH), bf1...  2.8 us

profile of v4, /device:TPU:17, one launch (start us, length us, event | category | flops | bytes accessed | tf_op | source)
XLA Modules:
  0.0 90.9 jit_solution(17110218953319985145)
XLA Ops:
  0.6 0.0 copy-start
  0.6 87.3 %gather_project.1 = (f32[7,896,256]{2,1,0:T(8,128)S(1)}, f32[896,128]{1,0:T(8,128)S(1)}, bf16[128,1792]{1,0:T(8,128)(2,1)S(1)}, f32[128,1792]{1,0:T(8,128)S(1)}) custom-call(bf16[896,512]{1,0:T(8,128)(2,1)} %tokens.1, bf16[128,1792]{1,0:T(8,128)(2,1)} %weight.1, bf16[1024,128]{1,0:T(8,128)(2,1)} %a_bank.1, bf16[1024,1792]{1,0:T(8,128)(2,1)} %b_bank.1, ...), custom_call_target="tpu_custom_call" | custom-call | tf_op jit(solution)/shard_map/gather_project/pallas_call | solution.py:454
  87.9 0.0 copy-done
  88.0 2.8 %finish.1 = (bf16[896,1792]{1,0:T(8,128)(2,1)}, f32[128,1792]{1,0:T(8,128)}) custom-call(f32[7,896,256]{2,1,0:T(8,128)S(1)} %get-tuple-element.6.acc, f32[896,128]{1,0:T(8,128)S(1)} %get-tuple-element.7.low, bf16[128,1792]{1,0:T(8,128)(2,1)S(1)} %get-tuple-element.8.own_b, f32[128,1792]{1,0:T(8,128)S(1)} %get-tuple-element.9.shaped, s32[2]{0:T(128)S(1)} %copy-done), custom_call_target="tpu_custom_call" | custom-call | tf_op jit(solution)/shard_map/finish/pallas_call | solution.py:491
Async XLA Ops:
  0.6 87.3 %copy-start = (s32[2]{0:T(128)S(1)}, s32[2]{0:T(128)}, u32[]{:S(2)}) copy-start(s32[2]{0:T(128)} %mirror.3) | copy-start | bytes 28
